TPU v7x, 32 devices: a whole 2x2x4 slice. The times are simulated.
32 devices in a mesh: cand: 2 (over y), hid: 16 (over z, x, core).
Axes of the slice: x: 2, y: 2, z: 4, core: 2. Of those that a mesh axis runs over, the one named last changes fastest.
Arguments:
- tokens: bfloat16 [32, 8192], P(('cand', 'hid')), parts along dimension 0, may hold values from -6 to 6
- teacher: bfloat16 [32, 8192], P(('cand', 'hid')), parts along dimension 0, may hold values from -4 to 4
- w_gate: bfloat16 [8192, 16384], P(None, 'hid'), may hold values from -0.0625 to 0.0625
- w_up: bfloat16 [8192, 16384], P(None, 'hid'), may hold values from -0.0625 to 0.0625
- w_down: bfloat16 [16384, 8192], P('hid'), may hold values from -0.046875 to 0.046875
- tile_scale: float32 [3, 128, 64], P(None, 'hid'), may hold values from 0.0005 to 0.005
- block_mask: int32 [6, 128, 64], P('cand', 'hid'), parts along dimension 0, may hold values from 0 to 1, as said below
- bit_width: int32 [6], P('cand'), parts along dimension 0, may hold values from 3 to 6
Outputs:
- student: bfloat16 [32, 8192], P(('cand', 'hid')), parts along dimension 0
- token_grad: bfloat16 [32, 8192], P(('cand', 'hid')), parts along dimension 0
- grad_gate: bfloat16 [16384, 16384], P('cand', 'hid'), parts along dimension 0
- grad_up: bfloat16 [16384, 16384], P('cand', 'hid'), parts along dimension 0
- grad_down: bfloat16 [32768, 8192], P(('cand', 'hid')), parts along dimension 0
There are 2 independent parts, one for each index of `cand`. A program takes and returns all parts, laid end to end along the dimension named above; an argument that names none is the same for every part. Nothing has to cross between parts.
Inputs may be any that keep to these rules, and one draw needn't show every extreme that they name: `block_mask`: each row of 64 width tiles of one matrix and hidden tile keeps 16 to 48 tiles; in every draw some row of each matrix keeps exactly 48.
All inputs are finite; a program needn't handle non-finite values.
Results may differ from a plain program's by a relative error of at most 0.0067.
Values may be sent and summed in bfloat16 or wider, within the bound.
A program may use at most 384 MiB of HBM per device.

v0:
```python
import functools

import jax
import jax.numpy as jnp
from jax import lax
from jax.experimental import pallas as pl
from jax.experimental.pallas import tpu as pltpu
from jax.sharding import PartitionSpec as P

BLOCK = 128
VMEM_BYTES = 56 * 1024 * 1024
F32 = jnp.float32
BF16 = jnp.bfloat16


def peer(index):
    return (lax.axis_index("cand"), index)


def greet(chips):
    me = lax.axis_index("hid")
    chip, core = me // 2, me % 2
    barrier = pltpu.get_barrier_semaphore()
    for k in range(1, chips):
        pl.semaphore_signal(
            barrier,
            inc=1,
            device_id=peer(2 * lax.rem(chip + k, chips) + core),
            device_id_type=pl.DeviceIdType.MESH,
        )
    pl.semaphore_signal(
        barrier, inc=1, device_id=peer(2 * chip + 1 - core), device_id_type=pl.DeviceIdType.MESH
    )
    pl.semaphore_wait(barrier, chips)


def remote(src, dst, send_sem, recv_sem, index):
    return pltpu.make_async_remote_copy(
        src_ref=src,
        dst_ref=dst,
        send_sem=send_sem,
        recv_sem=recv_sem,
        device_id=peer(index),
        device_id_type=pl.DeviceIdType.MESH,
    )


def gather_blocks(chips, held, far_send, far_recv, near_send, near_recv):
    me = lax.axis_index("hid")
    chip, core = me // 2, me % 2
    beside = 2 * chip + 1 - core
    started = []
    for k in range(1, chips):
        to = 2 * lax.rem(chip + k, chips) + core
        copy = remote(held.at[me], held.at[me], far_send.at[k], far_recv.at[k], to)
        copy.start()
        started.append(copy)
    own = remote(held.at[me], held.at[me], near_send.at[0], near_recv.at[0], beside)
    own.start()
    passed = [own]
    for k in range(1, chips):
        source = 2 * lax.rem(chip - k + chips, chips) + core
        arrived = remote(
            held.at[source], held.at[source], far_send.at[k], far_recv.at[k], source
        )
        arrived.wait_recv()
        onward = remote(
            held.at[source], held.at[source], near_send.at[k], near_recv.at[k], beside
        )
        onward.start()
        passed.append(onward)
    for k in range(chips):
        block = 2 * lax.rem(chip - k + chips, chips) + 1 - core
        remote(
            held.at[block], held.at[block], near_send.at[k], near_recv.at[k], beside
        ).wait_recv()
    for copy in started + passed:
        copy.wait_send()


def scatter_sum(chips, part, near_in, out_slot, far_in, far_send, far_recv, near_send, near_recv):
    me = lax.axis_index("hid")
    chip, core = me // 2, me % 2
    beside = 2 * chip + 1 - core
    near = []
    for k in range(1, chips + 1):
        to = lax.rem(chip + k, chips)
        copy = remote(
            part.at[1 - core, to], near_in.at[to], near_send.at[k - 1], near_recv.at[k - 1], beside
        )
        copy.start()
        near.append(copy)
    far = []
    for k in range(1, chips):
        to = lax.rem(chip + k, chips)
        near[k - 1].wait_recv()
        out_slot[k] = (part[core, to].astype(F32) + near_in[to].astype(F32)).astype(BF16)
        copy = remote(
            out_slot.at[k], far_in.at[k], far_send.at[k], far_recv.at[k], 2 * to + core
        )
        copy.start()
        far.append(copy)
    near[chips - 1].wait_recv()
    total = part[core, chip].astype(F32) + near_in[chip].astype(F32)
    for k in range(1, chips):
        far[k - 1].wait_recv()
        total = total + far_in[k].astype(F32)
    for copy in near + far:
        copy.wait_send()
    return total


def gather_kernel(chips, own, out, held, fs, fr, ns, nr):
    held[lax.axis_index("hid")] = own[...]
    greet(chips)
    gather_blocks(chips, held, fs, fr, ns, nr)
    out[...] = held[...]


def residual_kernel(
    chips, part, teacher, student, out, held, near_in, out_slot, far_in, fs, fr, ns, nr, fs2, fr2, ns2, nr2
):
    greet(chips)
    total = scatter_sum(chips, part, near_in, out_slot, far_in, fs, fr, ns, nr)
    student[...] = total.astype(BF16)
    held[lax.axis_index("hid")] = (total - teacher[...].astype(F32)).astype(BF16)
    gather_blocks(chips, held, fs2, fr2, ns2, nr2)
    out[...] = held[...]


def scatter_kernel(chips, part, out, near_in, out_slot, far_in, fs, fr, ns, nr):
    greet(chips)
    out[...] = scatter_sum(chips, part, near_in, out_slot, far_in, fs, fr, ns, nr).astype(BF16)


def link_sems(chips):
    return [pltpu.SemaphoreType.DMA((chips,))] * 4


def in_vmem(count):
    return [pl.BlockSpec(memory_space=pltpu.VMEM)] * count


def exchange(body, operands, out_shape, scratch, cid):
    return pl.pallas_call(
        body,
        out_shape=out_shape,
        in_specs=in_vmem(len(operands)),
        out_specs=jax.tree.map(lambda _: pl.BlockSpec(memory_space=pltpu.VMEM), out_shape),
        scratch_shapes=scratch,
        compiler_params=pltpu.CompilerParams(collective_id=cid, has_side_effects=True),
    )(*operands)


def contract_first(left, right):
    return lax.dot_general(
        left, right, (((0,), (0,)), ((), ())), preferred_element_type=F32
    )


def contract_last(left, right):
    return lax.dot_general(
        left, right, (((1,), (1,)), ((), ())), preferred_element_type=F32
    )


def one_hot(tiles, width):
    row = lax.broadcasted_iota(jnp.int32, (tiles, width), 0)
    column = lax.broadcasted_iota(jnp.int32, (tiles, width), 1)
    return (column // BLOCK == row).astype(F32).astype(BF16)


def spread_rows(tiles, into):
    count, per, wide = into.shape
    full = contract_first(tiles, one_hot(tiles.shape[0], wide))
    for g in range(count):
        into[g] = full[g * per : (g + 1) * per]


def spread_columns(tiles, into):
    count, per, wide = into.shape
    for g in range(count):
        cut = wide // BLOCK
        into[g] = jnp.dot(
            tiles[:, g * cut : (g + 1) * cut],
            one_hot(cut, wide),
            preferred_element_type=F32,
        )


def clipped(weight, bounds):
    pieces = []
    for j in range(weight.shape[0] // BLOCK):
        bound = bounds[j : j + 1].astype(BF16)
        piece = weight[j * BLOCK : (j + 1) * BLOCK]
        pieces.append(jnp.maximum(jnp.minimum(piece, bound), -bound))
    return jnp.concatenate(pieces, axis=0) if len(pieces) > 1 else pieces[0]


def to_rows(blocks, flat, into):
    tokens, tiles = blocks.shape[0], blocks.shape[1]
    flat[...] = blocks[...].astype(F32).reshape(flat.shape)
    count, _, wide = into.shape
    cut = wide // BLOCK
    for w in range(tiles):
        piece = flat[pl.ds(w, tokens, stride=tiles), :].astype(BF16)
        into[w // cut, :, (w % cut) * BLOCK : (w % cut + 1) * BLOCK] = piece


def put_columns(flat, value, first, tiles):
    tokens = value.shape[0]
    for j in range(value.shape[1] // BLOCK):
        flat[pl.ds(first + j, tokens, stride=tiles), :] = value[:, j * BLOCK : (j + 1) * BLOCK]


def to_shares(flat, out):
    _, chips, per, _ = out.shape
    for d in range(2 * chips):
        out[d % 2, d // 2] = flat[d * per : (d + 1) * per].astype(BF16)


def forward_kernel(
    steps, tiles, tok, wg, wu, wd, bound, part, gate_pre, up_pre, hidden, flat, rows, bg, bu, bd
):
    i = pl.program_id(0)

    @pl.when(i == 0)
    def _():
        to_rows(tok, flat, rows)
        spread_rows(bound[0], bg)
        spread_rows(bound[1], bu)
        spread_columns(bound[2], bd)
        gate_pre[...] = jnp.zeros_like(gate_pre)
        up_pre[...] = jnp.zeros_like(up_pre)

    @pl.when(i < steps)
    def _():
        gate_pre[...] += jnp.dot(rows[i], clipped(wg[...], bg[i]), preferred_element_type=F32)
        up_pre[...] += jnp.dot(rows[i], clipped(wu[...], bu[i]), preferred_element_type=F32)

    @pl.when(i == steps - 1)
    def _():
        gate = gate_pre[...]
        hidden[...] = (gate * jax.nn.sigmoid(gate) * up_pre[...]).astype(BF16)

    @pl.when(i >= steps)
    def _():
        c = i - steps
        value = jnp.dot(hidden[...], clipped(wd[...], bd[c]), preferred_element_type=F32)
        put_columns(flat, value, c * (value.shape[1] // BLOCK), tiles)

    @pl.when(i == 2 * steps - 1)
    def _():
        to_shares(flat, part)


def backward_kernel(
    steps, tiles, res, wg, wu, wd, bound, gate_pre, up_pre, part, d_gate, d_up, flat, rows, bg, bu, bd, d_hidden
):
    i = pl.program_id(0)

    @pl.when(i == 0)
    def _():
        to_rows(res, flat, rows)
        spread_rows(bound[0], bg)
        spread_rows(bound[1], bu)
        spread_columns(bound[2], bd)
        d_hidden[...] = jnp.zeros_like(d_hidden)

    @pl.when(i < steps)
    def _():
        d_hidden[...] += contract_last(rows[i], clipped(wd[...], bd[i]))

    @pl.when(i == steps - 1)
    def _():
        gate = gate_pre[...]
        sig = jax.nn.sigmoid(gate)
        d_gate[...] = (d_hidden[...] * up_pre[...] * sig * (1.0 + gate * (1.0 - sig))).astype(BF16)
        d_up[...] = (d_hidden[...] * (gate * sig)).astype(BF16)

    @pl.when(i >= steps)
    def _():
        c = i - steps
        value = contract_last(d_gate[...], clipped(wg[...], bg[c])) + contract_last(
            d_up[...], clipped(wu[...], bu[c])
        )
        put_columns(flat, value, c * (value.shape[1] // BLOCK), tiles)

    @pl.when(i == 2 * steps - 1)
    def _():
        to_shares(flat, part)


def outer(left, right, mask, out):
    for j in range(left.shape[1] // BLOCK):
        kept = right * mask[j : j + 1].astype(BF16)
        out[j * BLOCK : (j + 1) * BLOCK] = contract_first(
            left[:, j * BLOCK : (j + 1) * BLOCK], kept
        ).astype(BF16)


def grad_kernel(tok, res, hidden, d_gate, d_up, mask, gg, gu, gd, flat, rows, rows2, mg, mu, md):
    i = pl.program_id(0)

    @pl.when(i == 0)
    def _():
        to_rows(tok, flat, rows)
        to_rows(res, flat, rows2)
        spread_rows(mask[0], mg)
        spread_rows(mask[1], mu)
        spread_columns(mask[2], md)

    outer(rows[i], d_gate[...], mg[i], gg)
    outer(rows[i], d_up[...], mu[i], gu)
    outer(hidden[...], rows2[i], md[i], gd)


def per_device(n, tokens, teacher, w_gate, w_up, w_down, tile_scale, block_mask, bit_width):
    chips = n // 2
    mine, width = tokens.shape
    tiles = width // BLOCK
    all_tokens = n * mine
    hid = w_gate.shape[1]
    hid_tiles = hid // BLOCK
    cut = 512
    steps = width // cut
    per = cut // BLOCK
    share = mine * tiles

    level = (jnp.left_shift(1, bit_width - 1) - 1).astype(F32)
    mask = block_mask.astype(F32)
    bound = (tile_scale * level[:, None, None] * mask).astype(BF16)
    mask = mask.astype(BF16)

    block = jax.ShapeDtypeStruct((share, BLOCK), BF16)
    blocks = jax.ShapeDtypeStruct((n, share, BLOCK), BF16)
    held = pltpu.VMEM((n, share, BLOCK), BF16)
    some = pltpu.VMEM((chips, share, BLOCK), BF16)

    tok = exchange(
        functools.partial(gather_kernel, chips),
        (tokens.reshape(share, BLOCK),),
        blocks,
        [held] + link_sems(chips),
        0,
    ).reshape(all_tokens, tiles, BLOCK)

    whole = lambda shape: pl.BlockSpec(shape, lambda i: (0,) * len(shape))
    first = lambda i: jnp.minimum(i, steps - 1)
    second = lambda i: jnp.maximum(i - steps, 0)
    tok_spec = whole((all_tokens, tiles, BLOCK))
    pre_spec = whole((all_tokens, hid))
    part_shape = (2, chips, share, BLOCK)
    bound_spec = whole((3, hid_tiles, tiles))
    flat = pltpu.VMEM((all_tokens * tiles, BLOCK), F32)
    rows = pltpu.VMEM((steps, all_tokens, cut), BF16)
    row_tiles = pltpu.VMEM((steps, per, hid), F32)
    column_tiles = pltpu.VMEM((steps, hid_tiles, cut), F32)
    params = pltpu.CompilerParams(
        dimension_semantics=("arbitrary",), vmem_limit_bytes=VMEM_BYTES
    )
    pre = jax.ShapeDtypeStruct((all_tokens, hid), F32)
    low = jax.ShapeDtypeStruct((all_tokens, hid), BF16)

    part, gate_pre, up_pre, hidden = pl.pallas_call(
        functools.partial(forward_kernel, steps, tiles),
        grid=(2 * steps,),
        in_specs=[
            tok_spec,
            pl.BlockSpec((cut, hid), lambda i: (first(i), 0)),
            pl.BlockSpec((cut, hid), lambda i: (first(i), 0)),
            pl.BlockSpec((hid, cut), lambda i: (0, second(i))),
            bound_spec,
        ],
        out_specs=[whole(part_shape), pre_spec, pre_spec, pre_spec],
        out_shape=[jax.ShapeDtypeStruct(part_shape, BF16), pre, pre, low],
        scratch_shapes=[flat, rows, row_tiles, row_tiles, column_tiles],
        compiler_params=params,
    )(tok, w_gate, w_up, w_down, bound)

    student, res = exchange(
        functools.partial(residual_kernel, chips),
        (part, teacher.reshape(share, BLOCK)),
        (block, blocks),
        [held, some, some, some] + link_sems(chips) + link_sems(chips),
        1,
    )
    res = res.reshape(all_tokens, tiles, BLOCK)

    part, d_gate, d_up = pl.pallas_call(
        functools.partial(backward_kernel, steps, tiles),
        grid=(2 * steps,),
        in_specs=[
            tok_spec,
            pl.BlockSpec((cut, hid), lambda i: (second(i), 0)),
            pl.BlockSpec((cut, hid), lambda i: (second(i), 0)),
            pl.BlockSpec((hid, cut), lambda i: (0, first(i))),
            bound_spec,
            pre_spec,
            pre_spec,
        ],
        out_specs=[whole(part_shape), pre_spec, pre_spec],
        out_shape=[jax.ShapeDtypeStruct(part_shape, BF16), low, low],
        scratch_shapes=[
            flat, rows, row_tiles, row_tiles, column_tiles, pltpu.VMEM((all_tokens, hid), F32)
        ],
        compiler_params=params,
    )(res, w_gate, w_up, w_down, bound, gate_pre, up_pre)

    token_grad = exchange(
        functools.partial(scatter_kernel, chips),
        (part,),
        block,
        [some, some, some] + link_sems(chips),
        2,
    )

    grad_gate, grad_up, grad_down = pl.pallas_call(
        grad_kernel,
        grid=(steps,),
        in_specs=[tok_spec, tok_spec, pre_spec, pre_spec, pre_spec, bound_spec],
        out_specs=[
            pl.BlockSpec((cut, hid), lambda i: (i, 0)),
            pl.BlockSpec((cut, hid), lambda i: (i, 0)),
            pl.BlockSpec((hid, cut), lambda i: (0, i)),
        ],
        out_shape=[
            jax.ShapeDtypeStruct((width, hid), BF16),
            jax.ShapeDtypeStruct((width, hid), BF16),
            jax.ShapeDtypeStruct((hid, width), BF16),
        ],
        scratch_shapes=[flat, rows, rows, row_tiles, row_tiles, column_tiles],
        compiler_params=params,
    )(tok, res, hidden, d_gate, d_up, mask)

    return (
        student.reshape(mine, width),
        token_grad.reshape(mine, width),
        grad_gate,
        grad_up,
        grad_down,
    )


def solution(mesh):
    placed = (
        P(("cand", "hid"), None),
        P(("cand", "hid"), None),
        P(None, "hid"),
        P(None, "hid"),
        P("hid", None),
        P(None, "hid", None),
        P("cand", "hid", None),
        P("cand"),
    )
    return jax.shard_map(
        functools.partial(per_device, mesh.shape["hid"]),
        mesh=mesh,
        in_specs=placed,
        out_specs=(
            P(("cand", "hid"), None),
            P(("cand", "hid"), None),
            P("cand", "hid"),
            P("cand", "hid"),
            P(("cand", "hid"), None),
        ),
        check_vma=False,
    )
```

profile of v0, /device:TPU:0, one launch (start us, length us, event | category | flops | bytes accessed | tf_op | source)
XLA Modules:
  0.0 136.3 jit_solution(4856496835290705543)
XLA Ops:
  0.6 0.7 add_convert_fusion
  1.3 1.4 %multiply_convert_fusion.bound = bf16[3,8,64]{2,1,0:T(8,128)(2,1)} fusion(s32[3,8,64]{2,1,0:T(8,128)} %param.14, f32[3,8,64]{2,1,0:T(8,128)} %param.13, f32[3]{0:T(128)S(1)} %add_convert_fusion), kind=kLoop, calls=%fused_computation.2 | loop fusion | flops 6144 | bytes 15372 | tf_op jit(solution)/shard_map/convert_element_type | solution.py:332
  2.7 1.3 convert_convert_fusion.mask
  4.0 1.5 %reduce = bf16[8192]{0:T(1024)(128)(2,1)} reduce(bf16[1,8192]{1,0:T(2,128)(2,1)} %param.8, bf16[]{:T(256)} %constant.10), dimensions={0}, to_apply=%param.8.reduce_sub_computation | reduce | bytes 32770 | tf_op args[0]
  5.4 1.5 %reduce.1 = bf16[8192]{0:T(1024)(128)(2,1)} reduce(bf16[1,8192]{1,0:T(2,128)(2,1)} %param.9, bf16[]{:T(256)} %constant.10), dimensions={0}, to_apply=%param.9.reduce_sub_computation | reduce | bytes 32770 | tf_op args[1]
  6.9 11.8 %shard_map.119.tok = bf16[16,64,128]{2,1,0:T(8,128)(2,1)} custom-call(bf16[64,128]{1,0:T(8,128)(2,1)} %bitcast.11), custom_call_target="tpu_custom_call" | custom-call | tf_op jit(solution)/shard_map/pallas_call | solution.py:145
  18.7 32.2 %shard_map.120 = (bf16[2,8,64,128]{3,2,1,0:T(8,128)(2,1)}, f32[16,1024]{1,0:T(8,128)}, f32[16,1024]{1,0:T(8,128)}, bf16[16,1024]{1,0:T(8,128)(2,1)}) custom-call(bf16[16,64,128]{2,1,0:T(8,128)(2,1)} %shard_map.119.tok, bf16[8192,1024]{1,0:T(8,128)(2,1)} %wg.3, bf16[8192,1024]{1,0:T(8,128)(2,1)} %wu.3, bf16[1024,8192]{1,0:T(8,128)(2,1)} %wd.3, ...), custom_call_target="tpu_custom_call" | custom-call | tf_op jit(solution)/shard_map/pallas_call | solution.py:365
  50.9 18.1 %shard_map.121 = (bf16[64,128]{1,0:T(8,128)(2,1)}, bf16[16,64,128]{2,1,0:T(8,128)(2,1)}) custom-call(bf16[2,8,64,128]{3,2,1,0:T(8,128)(2,1)} %get-tuple-element.17.part, bf16[64,128]{1,0:T(8,128)(2,1)} %bitcast.10), custom_call_target="tpu_custom_call" | custom-call | tf_op jit(solution)/shard_map/pallas_call | solution.py:145
  69.0 0.0 copy-start
  69.0 34.8 %shard_map.122 = (bf16[2,8,64,128]{3,2,1,0:T(8,128)(2,1)}, bf16[16,1024]{1,0:T(8,128)(2,1)}, bf16[16,1024]{1,0:T(8,128)(2,1)}) custom-call(bf16[16,64,128]{2,1,0:T(8,128)(2,1)} %get-tuple-element.19.res, bf16[8192,1024]{1,0:T(8,128)(2,1)} %wg.3, bf16[8192,1024]{1,0:T(8,128)(2,1)} %wu.3, bf16[1024,8192]{1,0:T(8,128)(2,1)} %wd.3, ...), custom_call_target="tpu_custom_call" | custom-call | tf_op jit(solution)/shard_map/pallas_call | solution.py:390
  103.8 9.4 %shard_map.123 = bf16[64,128]{1,0:T(8,128)(2,1)} custom-call(bf16[2,8,64,128]{3,2,1,0:T(8,128)(2,1)} %get-tuple-element.22.part), custom_call_target="tpu_custom_call" | custom-call | tf_op jit(solution)/shard_map/pallas_call | solution.py:145
  113.2 0.0 copy-done
  113.2 1.4 %copy_bitcast_fusion = (bf16[1,8192]{1,0:T(2,128)(2,1)}, bf16[1,8192]{1,0:T(2,128)(2,1)}) fusion(bf16[1,1,64,128]{3,2,1,0:T(8,128)(2,1)} %bitcast.12, bf16[1,1,64,128]{3,2,1,0:T(8,128)(2,1)S(1)} %bitcast.13), kind=kLoop, calls=%fused_computation | loop fusion | bytes 65536 | tf_op jit(solution)/shard_map/reshape | solution.py:438
  114.6 21.8 %shard_map.124 = (bf16[8192,1024]{1,0:T(8,128)(2,1)}, bf16[8192,1024]{1,0:T(8,128)(2,1)}, bf16[1024,8192]{1,0:T(8,128)(2,1)}) custom-call(bf16[16,64,128]{2,1,0:T(8,128)(2,1)} %shard_map.119.tok, bf16[16,64,128]{2,1,0:T(8,128)(2,1)} %get-tuple-element.19.res, bf16[16,1024]{1,0:T(8,128)(2,1)} %get-tuple-element.23.hidden, ...), custom_call_target="tpu_custom_call" | custom-call | tf_op jit(solution)/shard_map/pallas_call | solution.py:418
Async XLA Ops:
  69.0 44.2 %copy-start = (bf16[64,128]{1,0:T(8,128)(2,1)S(1)}, bf16[64,128]{1,0:T(8,128)(2,1)}, u32[]{:S(2)}) copy-start(bf16[64,128]{1,0:T(8,128)(2,1)} %get-tuple-element.18) | copy-start | bytes 49156
where the time goes:
time: 138 us; the launch traced here: 136 us
  Pallas kernels  128 us (93%)
  other arithmetic  6.24 us (5%)
  local copies, waits for them, and re-layouts  1.4 us (1%)
    pallas_call x3, Pallas kernels, exchange(): pl.pallas_call(body, out_shape=out_shape, in_specs=in_vmem(len(operands))...  39.3 us
    pallas_call x1, Pallas kernels, per_device(): pl.pallas_call(functools.partial(backward_kernel, steps, tiles), grid=(2...  34.8 us
    pallas_call x1, Pallas kernels, per_device(): pl.pallas_call(functools.partial(forward_kernel, steps, tiles), grid=(2 *...  32.2 us
    pallas_call x1, Pallas kernels, per_device(): pl.pallas_call(grad_kernel, grid=(steps,), in_specs=[tok_spec, tok_spec,...  21.8 us
    unnamed x2, other arithmetic  2.9 us

commit v1 on v0

--- a/solution.py
+++ b/solution.py
@@ -8,9 +8,10 @@
 from jax.sharding import PartitionSpec as P
 
 BLOCK = 128
-VMEM_BYTES = 56 * 1024 * 1024
+VMEM_BYTES = 60 * 1024 * 1024
 F32 = jnp.float32
 BF16 = jnp.bfloat16
+AHEAD = 3
 
 
 def peer(index):
@@ -110,27 +111,31 @@
     return total
 
 
-def gather_kernel(chips, own, out, held, fs, fr, ns, nr):
-    held[lax.axis_index("hid")] = own[...]
+def gather_kernel(chips, own, out, held, line, fs, fr, ns, nr):
+    unroll_tokens(own[...].astype(F32), line)
+    held[lax.axis_index("hid")] = line[...].astype(BF16)
     greet(chips)
     gather_blocks(chips, held, fs, fr, ns, nr)
     out[...] = held[...]
 
 
 def residual_kernel(
-    chips, part, teacher, student, out, held, near_in, out_slot, far_in, fs, fr, ns, nr, fs2, fr2, ns2, nr2
+    chips, part, teacher, student, out, held, near_in, out_slot, far_in, line, fs, fr, ns, nr, fs2, fr2, ns2, nr2
 ):
     greet(chips)
     total = scatter_sum(chips, part, near_in, out_slot, far_in, fs, fr, ns, nr)
-    student[...] = total.astype(BF16)
-    held[lax.axis_index("hid")] = (total - teacher[...].astype(F32)).astype(BF16)
+    unroll_tokens(teacher[...].astype(F32), line)
+    held[lax.axis_index("hid")] = (total - line[...]).astype(BF16)
+    line[...] = total
+    roll_tokens(line, student)
     gather_blocks(chips, held, fs2, fr2, ns2, nr2)
     out[...] = held[...]
 
 
-def scatter_kernel(chips, part, out, near_in, out_slot, far_in, fs, fr, ns, nr):
+def scatter_kernel(chips, part, out, near_in, out_slot, far_in, line, fs, fr, ns, nr):
     greet(chips)
-    out[...] = scatter_sum(chips, part, near_in, out_slot, far_in, fs, fr, ns, nr).astype(BF16)
+    line[...] = scatter_sum(chips, part, near_in, out_slot, far_in, fs, fr, ns, nr)
+    roll_tokens(line, out)
 
 
 def link_sems(chips):
@@ -219,76 +224,175 @@
         out[d % 2, d // 2] = flat[d * per : (d + 1) * per].astype(BF16)
 
 
+def bounds_of(scale, mask, width, bg, bu, bd):
+    for m, into in enumerate((bg, bu, bd)):
+        level = (jnp.left_shift(1, width[m] - 1) - 1).astype(F32)
+        tiles = (scale[m] * level * mask[m].astype(F32)).astype(BF16)
+        if m < 2:
+            spread_rows(tiles, into)
+        else:
+            spread_columns(tiles, into)
+
+
+def in_pairs(steps, cut, wg, wu, gate_w, up_w, sems, i):
+    rows = pl.ds(pl.multiple_of(i * cut, cut), cut)
+    return (
+        pltpu.make_async_copy(wg.at[rows], gate_w.at[i], sems.at[0, i]),
+        pltpu.make_async_copy(wu.at[rows], up_w.at[i], sems.at[1, i]),
+    )
+
+
+def in_down(steps, cut, wd, down_w, sems, i):
+    columns = pl.ds(pl.multiple_of(i * cut, cut), cut)
+    return pltpu.make_async_copy(wd.at[:, columns], down_w.at[i], sems.at[2, i])
+
+
+def unroll_tokens(tokens, flat):
+    count, width = tokens.shape
+    tiles = width // BLOCK
+    for t in range(count):
+        for w in range(tiles):
+            flat[t * tiles + w : t * tiles + w + 1, :] = tokens[
+                t : t + 1, w * BLOCK : (w + 1) * BLOCK
+            ]
+
+
+def roll_tokens(flat, out):
+    count, width = out.shape
+    tiles = width // BLOCK
+    for w in range(tiles):
+        pieces = [flat[t * tiles + w : t * tiles + w + 1, :] for t in range(count)]
+        piece = jnp.concatenate(pieces, axis=0) if count > 1 else pieces[0]
+        out[:, w * BLOCK : (w + 1) * BLOCK] = piece.astype(BF16)
+
+
+def start_all(copies):
+    for copy in copies:
+        copy.start()
+
+
+def forward_products(
+    steps, cut, tiles, rows, weights, held_w, sems, bg, bu, bd, gate_pre, up_pre, hidden, flat, keep
+):
+    wg, wu, wd = weights
+    gate_w, up_w, down_w = held_w
+    pair = functools.partial(in_pairs, steps, cut, wg, wu, gate_w, up_w, sems)
+    down = functools.partial(in_down, steps, cut, wd, down_w, sems)
+    ahead = min(AHEAD, steps)
+    gate_pre[...] = jnp.zeros_like(gate_pre)
+    up_pre[...] = jnp.zeros_like(up_pre)
+
+    @pl.loop(0, steps)
+    def _(i):
+        @pl.when(i + ahead < steps)
+        def _():
+            start_all(pair(i + ahead))
+
+        @pl.when(i + ahead >= steps)
+        def _():
+            start_all([down(2 * (i + ahead - steps)), down(2 * (i + ahead - steps) + 1)])
+
+        for copy in pair(i):
+            copy.wait()
+        for source, bound, into in ((gate_w, bg, gate_pre), (up_w, bu, up_pre)):
+            value = clipped(source[i], bound[i])
+            if keep:
+                source[i] = value
+            into[...] += jnp.dot(rows[i], value, preferred_element_type=F32)
+
+    gate = gate_pre[...]
+    hidden[...] = (gate * jax.nn.sigmoid(gate) * up_pre[...]).astype(BF16)
+
+    @pl.loop(0, steps)
+    def _(c):
+        @pl.when(c + 2 * ahead < steps)
+        def _():
+            down(c + 2 * ahead).start()
+
+        down(c).wait()
+        kept = clipped(down_w[c], bd[c])
+        if keep:
+            down_w[c] = kept
+        value = jnp.dot(hidden[...], kept, preferred_element_type=F32)
+        put_columns(flat, value, c * (cut // BLOCK), tiles)
+
+
+def backward_products(
+    steps, cut, tiles, rows, held_w, gate_pre, up_pre, d_hidden, d_gate, d_up, flat, ready_down, ready_pair
+):
+    gate_w, up_w, down_w = held_w
+    d_hidden[...] = jnp.zeros_like(d_hidden)
+
+    @pl.loop(0, steps)
+    def _(c):
+        d_hidden[...] += contract_last(rows[c], ready_down(c))
+
+    gate = gate_pre[...]
+    sig = jax.nn.sigmoid(gate)
+    d_gate[...] = (d_hidden[...] * up_pre[...] * sig * (1.0 + gate * (1.0 - sig))).astype(BF16)
+    d_up[...] = (d_hidden[...] * (gate * sig)).astype(BF16)
+
+    @pl.loop(0, steps)
+    def _(i):
+        gate_i, up_i = ready_pair(i)
+        value = contract_last(d_gate[...], gate_i) + contract_last(d_up[...], up_i)
+        put_columns(flat, value, i * (cut // BLOCK), tiles)
+
+
 def forward_kernel(
-    steps, tiles, tok, wg, wu, wd, bound, part, gate_pre, up_pre, hidden, flat, rows, bg, bu, bd
+    steps, cut, tiles, width, tok, wg, wu, wd, scale, mask, part, gate_pre, up_pre, hidden,
+    flat, rows, bg, bu, bd, gate_w, up_w, down_w, sems
 ):
-    i = pl.program_id(0)
-
-    @pl.when(i == 0)
-    def _():
-        to_rows(tok, flat, rows)
-        spread_rows(bound[0], bg)
-        spread_rows(bound[1], bu)
-        spread_columns(bound[2], bd)
-        gate_pre[...] = jnp.zeros_like(gate_pre)
-        up_pre[...] = jnp.zeros_like(up_pre)
-
-    @pl.when(i < steps)
-    def _():
-        gate_pre[...] += jnp.dot(rows[i], clipped(wg[...], bg[i]), preferred_element_type=F32)
-        up_pre[...] += jnp.dot(rows[i], clipped(wu[...], bu[i]), preferred_element_type=F32)
-
-    @pl.when(i == steps - 1)
-    def _():
-        gate = gate_pre[...]
-        hidden[...] = (gate * jax.nn.sigmoid(gate) * up_pre[...]).astype(BF16)
-
-    @pl.when(i >= steps)
-    def _():
-        c = i - steps
-        value = jnp.dot(hidden[...], clipped(wd[...], bd[c]), preferred_element_type=F32)
-        put_columns(flat, value, c * (value.shape[1] // BLOCK), tiles)
-
-    @pl.when(i == 2 * steps - 1)
-    def _():
-        to_shares(flat, part)
+    held_w = (gate_w, up_w, down_w)
+    for i in range(min(AHEAD, steps)):
+        start_all(in_pairs(steps, cut, wg, wu, gate_w, up_w, sems, i))
+    to_rows(tok, flat, rows)
+    bounds_of(scale, mask, width, bg, bu, bd)
+    forward_products(
+        steps, cut, tiles, rows, (wg, wu, wd), held_w, sems, bg, bu, bd,
+        gate_pre, up_pre, hidden, flat, False,
+    )
+    to_shares(flat, part)
 
 
 def backward_kernel(
-    steps, tiles, res, wg, wu, wd, bound, gate_pre, up_pre, part, d_gate, d_up, flat, rows, bg, bu, bd, d_hidden
+    steps, cut, tiles, width, res, wg, wu, wd, scale, mask, gate_pre, up_pre, part, d_gate, d_up,
+    flat, rows, bg, bu, bd, gate_w, up_w, down_w, sems, d_hidden
 ):
-    i = pl.program_id(0)
-
-    @pl.when(i == 0)
-    def _():
-        to_rows(res, flat, rows)
-        spread_rows(bound[0], bg)
-        spread_rows(bound[1], bu)
-        spread_columns(bound[2], bd)
-        d_hidden[...] = jnp.zeros_like(d_hidden)
-
-    @pl.when(i < steps)
-    def _():
-        d_hidden[...] += contract_last(rows[i], clipped(wd[...], bd[i]))
-
-    @pl.when(i == steps - 1)
-    def _():
-        gate = gate_pre[...]
-        sig = jax.nn.sigmoid(gate)
-        d_gate[...] = (d_hidden[...] * up_pre[...] * sig * (1.0 + gate * (1.0 - sig))).astype(BF16)
-        d_up[...] = (d_hidden[...] * (gate * sig)).astype(BF16)
-
-    @pl.when(i >= steps)
-    def _():
-        c = i - steps
-        value = contract_last(d_gate[...], clipped(wg[...], bg[c])) + contract_last(
-            d_up[...], clipped(wu[...], bu[c])
-        )
-        put_columns(flat, value, c * (value.shape[1] // BLOCK), tiles)
-
-    @pl.when(i == 2 * steps - 1)
-    def _():
-        to_shares(flat, part)
+    pair = functools.partial(in_pairs, steps, cut, wg, wu, gate_w, up_w, sems)
+    down = functools.partial(in_down, steps, cut, wd, down_w, sems)
+    ahead = min(2 * AHEAD, steps)
+    for c in range(ahead):
+        down(c).start()
+    to_rows(res, flat, rows)
+    bounds_of(scale, mask, width, bg, bu, bd)
+
+    def ready_down(c):
+        @pl.when(c + ahead < steps)
+        def _():
+            down(c + ahead).start()
+
+        @pl.when(c + ahead >= steps)
+        def _():
+            start_all(pair(c + ahead - steps))
+
+        down(c).wait()
+        return clipped(down_w[c], bd[c])
+
+    def ready_pair(i):
+        @pl.when(i + ahead < steps)
+        def _():
+            start_all(pair(i + ahead))
+
+        for copy in pair(i):
+            copy.wait()
+        return clipped(gate_w[i], bg[i]), clipped(up_w[i], bu[i])
+
+    backward_products(
+        steps, cut, tiles, rows, (gate_w, up_w, down_w), gate_pre, up_pre, d_hidden, d_gate, d_up,
+        flat, ready_down, ready_pair,
+    )
+    to_shares(flat, part)
 
 
 def outer(left, right, mask, out):
@@ -306,9 +410,9 @@
     def _():
         to_rows(tok, flat, rows)
         to_rows(res, flat, rows2)
-        spread_rows(mask[0], mg)
-        spread_rows(mask[1], mu)
-        spread_columns(mask[2], md)
+        spread_rows(mask[0].astype(F32).astype(BF16), mg)
+        spread_rows(mask[1].astype(F32).astype(BF16), mu)
+        spread_columns(mask[2].astype(F32).astype(BF16), md)
 
     outer(rows[i], d_gate[...], mg[i], gg)
     outer(rows[i], d_up[...], mu[i], gu)
@@ -322,32 +426,26 @@
     all_tokens = n * mine
     hid = w_gate.shape[1]
     hid_tiles = hid // BLOCK
-    cut = 512
+    cut = 1024
     steps = width // cut
     per = cut // BLOCK
     share = mine * tiles
 
-    level = (jnp.left_shift(1, bit_width - 1) - 1).astype(F32)
-    mask = block_mask.astype(F32)
-    bound = (tile_scale * level[:, None, None] * mask).astype(BF16)
-    mask = mask.astype(BF16)
-
-    block = jax.ShapeDtypeStruct((share, BLOCK), BF16)
+    block = jax.ShapeDtypeStruct((mine, width), BF16)
+    line = pltpu.VMEM((share, BLOCK), F32)
     blocks = jax.ShapeDtypeStruct((n, share, BLOCK), BF16)
     held = pltpu.VMEM((n, share, BLOCK), BF16)
     some = pltpu.VMEM((chips, share, BLOCK), BF16)
 
     tok = exchange(
         functools.partial(gather_kernel, chips),
-        (tokens.reshape(share, BLOCK),),
+        (tokens,),
         blocks,
-        [held] + link_sems(chips),
+        [held, line] + link_sems(chips),
         0,
     ).reshape(all_tokens, tiles, BLOCK)
 
     whole = lambda shape: pl.BlockSpec(shape, lambda i: (0,) * len(shape))
-    first = lambda i: jnp.minimum(i, steps - 1)
-    second = lambda i: jnp.maximum(i - steps, 0)
     tok_spec = whole((all_tokens, tiles, BLOCK))
     pre_spec = whole((all_tokens, hid))
     part_shape = (2, chips, share, BLOCK)
@@ -362,56 +460,50 @@
     pre = jax.ShapeDtypeStruct((all_tokens, hid), F32)
     low = jax.ShapeDtypeStruct((all_tokens, hid), BF16)
 
+    anywhere = pl.BlockSpec(memory_space=pl.ANY)
+    vmem = pl.BlockSpec(memory_space=pltpu.VMEM)
+    smem = pl.BlockSpec(memory_space=pltpu.SMEM)
+    plain = pltpu.CompilerParams(vmem_limit_bytes=VMEM_BYTES)
+    stores = [
+        pltpu.VMEM((steps, cut, hid), BF16),
+        pltpu.VMEM((steps, cut, hid), BF16),
+        pltpu.VMEM((steps, hid, cut), BF16),
+        pltpu.SemaphoreType.DMA((3, steps)),
+    ]
     part, gate_pre, up_pre, hidden = pl.pallas_call(
-        functools.partial(forward_kernel, steps, tiles),
-        grid=(2 * steps,),
-        in_specs=[
-            tok_spec,
-            pl.BlockSpec((cut, hid), lambda i: (first(i), 0)),
-            pl.BlockSpec((cut, hid), lambda i: (first(i), 0)),
-            pl.BlockSpec((hid, cut), lambda i: (0, second(i))),
-            bound_spec,
-        ],
-        out_specs=[whole(part_shape), pre_spec, pre_spec, pre_spec],
+        functools.partial(forward_kernel, steps, cut, tiles),
+        in_specs=[smem, vmem, anywhere, anywhere, anywhere, vmem, vmem],
+        out_specs=[vmem] * 4,
         out_shape=[jax.ShapeDtypeStruct(part_shape, BF16), pre, pre, low],
-        scratch_shapes=[flat, rows, row_tiles, row_tiles, column_tiles],
-        compiler_params=params,
-    )(tok, w_gate, w_up, w_down, bound)
+        scratch_shapes=[flat, rows, row_tiles, row_tiles, column_tiles] + stores,
+        compiler_params=plain,
+    )(bit_width, tok, w_gate, w_up, w_down, tile_scale, block_mask)
 
     student, res = exchange(
         functools.partial(residual_kernel, chips),
-        (part, teacher.reshape(share, BLOCK)),
+        (part, teacher),
         (block, blocks),
-        [held, some, some, some] + link_sems(chips) + link_sems(chips),
+        [held, some, some, some, line] + link_sems(chips) + link_sems(chips),
         1,
     )
     res = res.reshape(all_tokens, tiles, BLOCK)
 
     part, d_gate, d_up = pl.pallas_call(
-        functools.partial(backward_kernel, steps, tiles),
-        grid=(2 * steps,),
-        in_specs=[
-            tok_spec,
-            pl.BlockSpec((cut, hid), lambda i: (second(i), 0)),
-            pl.BlockSpec((cut, hid), lambda i: (second(i), 0)),
-            pl.BlockSpec((hid, cut), lambda i: (0, first(i))),
-            bound_spec,
-            pre_spec,
-            pre_spec,
-        ],
-        out_specs=[whole(part_shape), pre_spec, pre_spec],
+        functools.partial(backward_kernel, steps, cut, tiles),
+        in_specs=[smem, vmem, anywhere, anywhere, anywhere, vmem, vmem, vmem, vmem],
+        out_specs=[vmem] * 3,
         out_shape=[jax.ShapeDtypeStruct(part_shape, BF16), low, low],
-        scratch_shapes=[
-            flat, rows, row_tiles, row_tiles, column_tiles, pltpu.VMEM((all_tokens, hid), F32)
-        ],
-        compiler_params=params,
-    )(res, w_gate, w_up, w_down, bound, gate_pre, up_pre)
+        scratch_shapes=[flat, rows, row_tiles, row_tiles, column_tiles]
+        + stores
+        + [pltpu.VMEM((all_tokens, hid), F32)],
+        compiler_params=plain,
+    )(bit_width, res, w_gate, w_up, w_down, tile_scale, block_mask, gate_pre, up_pre)
 
     token_grad = exchange(
         functools.partial(scatter_kernel, chips),
         (part,),
         block,
-        [some, some, some] + link_sems(chips),
+        [some, some, some, line] + link_sems(chips),
         2,
     )
 
@@ -431,11 +523,11 @@
         ],
         scratch_shapes=[flat, rows, rows, row_tiles, row_tiles, column_tiles],
         compiler_params=params,
-    )(tok, res, hidden, d_gate, d_up, mask)
+    )(tok, res, hidden, d_gate, d_up, block_mask)
 
     return (
-        student.reshape(mine, width),
-        token_grad.reshape(mine, width),
+        student,
+        token_grad,
         grad_gate,
         grad_up,
         grad_down,

time: 138 us -> 99.2 us (0.72)
  Pallas kernels: 128 us -> 96.2 us
  other arithmetic: 6.24 us -> 0 us
    pallas_call x2, Pallas kernels: 67 us -> 37.2 us  [the longest x1 19.1 us: per_device(): pl.pallas_call(functools.partial(backward_kernel, steps, cut, tiles), in_...]
    convert_element_type x3 -> x0, other arithmetic: 3.34 us -> none  [the longest x1 1.37 us: per_device(): bound = (tile_scale * level[:, None, None] * mask).astype(BF16)]
    unnamed x2 -> x0, other arithmetic: 2.9 us -> none
    pallas_call x1, Pallas kernels: 21.8 us -> 19.5 us  [per_device(): pl.pallas_call(grad_kernel, grid=(steps,), in_specs=[tok_spec, tok_spec,...]
    unnamed x2 -> x4, local copies, waits for them, and re-layouts: 0.01 us -> 2.02 us
    reshape x1 -> x0, local copies, waits for them, and re-layouts: 1.39 us -> none  [per_device(): token_grad.reshape(mine, width)]
where the time goes in v1:
time: 99.2 us; the launch traced here: 98.9 us
  Pallas kernels  96.2 us (97%)
  local copies, waits for them, and re-layouts  2.02 us (2%)
    pallas_call x3, Pallas kernels, exchange(): pl.pallas_call(body, out_shape=out_shape, in_specs=in_vmem(len(operands))...  39.5 us
    pallas_call x1, Pallas kernels, per_device(): pl.pallas_call(grad_kernel, grid=(steps,), in_specs=[tok_spec, tok_spec,...  19.5 us
    pallas_call x1, Pallas kernels, per_device(): pl.pallas_call(functools.partial(backward_kernel, steps, cut, tiles), in_...  19.1 us
    pallas_call x1, Pallas kernels, per_device(): pl.pallas_call(functools.partial(forward_kernel, steps, cut, tiles), in_s...  18 us
    unnamed x4, local copies, waits for them, and re-layouts  2.02 us

profile of v1, /device:TPU:0, one launch (start us, length us, event | category | flops | bytes accessed | tf_op | source)
XLA Modules:
  0.0 98.9 jit_solution(5284412928446269676)
XLA Ops:
  0.6 12.0 %shard_map.119.tok = bf16[16,64,128]{2,1,0:T(8,128)(2,1)} custom-call(bf16[1,8192]{1,0:T(2,128)(2,1)} %own.1), custom_call_target="tpu_custom_call" | custom-call | tf_op jit(solution)/shard_map/pallas_call | solution.py:150
  12.6 18.0 %shard_map.120 = (bf16[2,8,64,128]{3,2,1,0:T(8,128)(2,1)}, f32[16,1024]{1,0:T(8,128)}, f32[16,1024]{1,0:T(8,128)}, bf16[16,1024]{1,0:T(8,128)(2,1)}) custom-call(s32[3]{0:T(128)} %width.3, bf16[16,64,128]{2,1,0:T(8,128)(2,1)} %shard_map.119.tok, bf16[8192,1024]{1,0:T(8,128)(2,1)} %wg.3, bf16[8192,1024]{1,0:T(8,128)(2,1)} %wu.3, bf16[1024,8192]{1,0:T(8,128)(2,1)} %wd.3, ...), custom_call_target="tpu_custom_call" | custom-call | tf_op jit(solution)/shard_map/pallas_call | solution.py:473
  30.7 18.1 %shard_map.121 = (bf16[1,8192]{1,0:T(2,128)(2,1)}, bf16[16,64,128]{2,1,0:T(8,128)(2,1)}) custom-call(bf16[2,8,64,128]{3,2,1,0:T(8,128)(2,1)} %get-tuple-element.17.part, bf16[1,8192]{1,0:T(2,128)(2,1)} %teacher.1), custom_call_target="tpu_custom_call" | custom-call | tf_op jit(solution)/shard_map/pallas_call | solution.py:150
  48.8 0.0 copy-start
  48.8 19.1 %shard_map.122 = (bf16[2,8,64,128]{3,2,1,0:T(8,128)(2,1)}, bf16[16,1024]{1,0:T(8,128)(2,1)}, bf16[16,1024]{1,0:T(8,128)(2,1)}) custom-call(s32[3]{0:T(128)} %width.3, bf16[16,64,128]{2,1,0:T(8,128)(2,1)} %get-tuple-element.19.res, bf16[8192,1024]{1,0:T(8,128)(2,1)} %wg.3, bf16[8192,1024]{1,0:T(8,128)(2,1)} %wu.3, bf16[1024,8192]{1,0:T(8,128)(2,1)} %wd.3, ...), custom_call_target="tpu_custom_call" | custom-call | tf_op jit(solution)/shard_map/pallas_call | solution.py:491
  67.9 9.4 %shard_map.123 = bf16[1,8192]{1,0:T(2,128)(2,1)} custom-call(bf16[2,8,64,128]{3,2,1,0:T(8,128)(2,1)} %get-tuple-element.22.part), custom_call_target="tpu_custom_call" | custom-call | tf_op jit(solution)/shard_map/pallas_call | solution.py:150
  77.4 19.5 %shard_map.124 = (bf16[8192,1024]{1,0:T(8,128)(2,1)}, bf16[8192,1024]{1,0:T(8,128)(2,1)}, bf16[1024,8192]{1,0:T(8,128)(2,1)}) custom-call(bf16[16,64,128]{2,1,0:T(8,128)(2,1)} %shard_map.119.tok, bf16[16,64,128]{2,1,0:T(8,128)(2,1)} %get-tuple-element.19.res, bf16[16,1024]{1,0:T(8,128)(2,1)} %get-tuple-element.23.hidden, ...), custom_call_target="tpu_custom_call" | custom-call | tf_op jit(solution)/shard_map/pallas_call | solution.py:510
  96.9 0.0 copy-done
  96.9 0.6 copy.15
  97.5 1.4 %copy.16 = bf16[1,8192]{1,0:T(2,128)(2,1)} copy(bf16[1,8192]{1,0:T(2,128)(2,1)} %shard_map.123) | data formatting | bytes 32768
Async XLA Ops:
  48.8 48.1 %copy-start = (bf16[1,8192]{1,0:T(2,128)(2,1)S(1)}, bf16[1,8192]{1,0:T(2,128)(2,1)}, u32[]{:S(2)}) copy-start(bf16[1,8192]{1,0:T(2,128)(2,1)} %get-tuple-element.34) | copy-start | bytes 49156

commit v2 on v1

--- a/solution.py
+++ b/solution.py
@@ -111,50 +111,8 @@
     return total
 
 
-def gather_kernel(chips, own, out, held, line, fs, fr, ns, nr):
-    unroll_tokens(own[...].astype(F32), line)
-    held[lax.axis_index("hid")] = line[...].astype(BF16)
-    greet(chips)
-    gather_blocks(chips, held, fs, fr, ns, nr)
-    out[...] = held[...]
-
-
-def residual_kernel(
-    chips, part, teacher, student, out, held, near_in, out_slot, far_in, line, fs, fr, ns, nr, fs2, fr2, ns2, nr2
-):
-    greet(chips)
-    total = scatter_sum(chips, part, near_in, out_slot, far_in, fs, fr, ns, nr)
-    unroll_tokens(teacher[...].astype(F32), line)
-    held[lax.axis_index("hid")] = (total - line[...]).astype(BF16)
-    line[...] = total
-    roll_tokens(line, student)
-    gather_blocks(chips, held, fs2, fr2, ns2, nr2)
-    out[...] = held[...]
-
-
-def scatter_kernel(chips, part, out, near_in, out_slot, far_in, line, fs, fr, ns, nr):
-    greet(chips)
-    line[...] = scatter_sum(chips, part, near_in, out_slot, far_in, fs, fr, ns, nr)
-    roll_tokens(line, out)
-
-
 def link_sems(chips):
     return [pltpu.SemaphoreType.DMA((chips,))] * 4
-
-
-def in_vmem(count):
-    return [pl.BlockSpec(memory_space=pltpu.VMEM)] * count
-
-
-def exchange(body, operands, out_shape, scratch, cid):
-    return pl.pallas_call(
-        body,
-        out_shape=out_shape,
-        in_specs=in_vmem(len(operands)),
-        out_specs=jax.tree.map(lambda _: pl.BlockSpec(memory_space=pltpu.VMEM), out_shape),
-        scratch_shapes=scratch,
-        compiler_params=pltpu.CompilerParams(collective_id=cid, has_side_effects=True),
-    )(*operands)
 
 
 def contract_first(left, right):
@@ -203,9 +161,9 @@
 
 
 def to_rows(blocks, flat, into):
-    tokens, tiles = blocks.shape[0], blocks.shape[1]
     flat[...] = blocks[...].astype(F32).reshape(flat.shape)
-    count, _, wide = into.shape
+    count, tokens, wide = into.shape
+    tiles = count * wide // BLOCK
     cut = wide // BLOCK
     for w in range(tiles):
         piece = flat[pl.ds(w, tokens, stride=tiles), :].astype(BF16)
@@ -339,60 +297,41 @@
         put_columns(flat, value, i * (cut // BLOCK), tiles)
 
 
-def forward_kernel(
-    steps, cut, tiles, width, tok, wg, wu, wd, scale, mask, part, gate_pre, up_pre, hidden,
-    flat, rows, bg, bu, bd, gate_w, up_w, down_w, sems
+def layer_kernel(
+    chips, steps, cut, tiles, width, tokens, teacher, wg, wu, wd, scale, mask,
+    student, token_grad, rows, res_rows, hidden, d_gate, d_up,
+    gate_w, up_w, down_w, sems, flat, bg, bu, bd, gate_pre, up_pre, d_hidden, line, part,
+    tok_held, near_1, slot_1, far_1, res_held, near_2, slot_2, far_2, *links
 ):
     held_w = (gate_w, up_w, down_w)
     for i in range(min(AHEAD, steps)):
         start_all(in_pairs(steps, cut, wg, wu, gate_w, up_w, sems, i))
-    to_rows(tok, flat, rows)
+    unroll_tokens(tokens[...].astype(F32), line)
+    tok_held[lax.axis_index("hid")] = line[...].astype(BF16)
+    greet(chips)
     bounds_of(scale, mask, width, bg, bu, bd)
+    gather_blocks(chips, tok_held, *links[0:4])
+    to_rows(tok_held, flat, rows)
     forward_products(
         steps, cut, tiles, rows, (wg, wu, wd), held_w, sems, bg, bu, bd,
-        gate_pre, up_pre, hidden, flat, False,
+        gate_pre, up_pre, hidden, flat, True,
     )
     to_shares(flat, part)
-
-
-def backward_kernel(
-    steps, cut, tiles, width, res, wg, wu, wd, scale, mask, gate_pre, up_pre, part, d_gate, d_up,
-    flat, rows, bg, bu, bd, gate_w, up_w, down_w, sems, d_hidden
-):
-    pair = functools.partial(in_pairs, steps, cut, wg, wu, gate_w, up_w, sems)
-    down = functools.partial(in_down, steps, cut, wd, down_w, sems)
-    ahead = min(2 * AHEAD, steps)
-    for c in range(ahead):
-        down(c).start()
-    to_rows(res, flat, rows)
-    bounds_of(scale, mask, width, bg, bu, bd)
-
-    def ready_down(c):
-        @pl.when(c + ahead < steps)
-        def _():
-            down(c + ahead).start()
-
-        @pl.when(c + ahead >= steps)
-        def _():
-            start_all(pair(c + ahead - steps))
-
-        down(c).wait()
-        return clipped(down_w[c], bd[c])
-
-    def ready_pair(i):
-        @pl.when(i + ahead < steps)
-        def _():
-            start_all(pair(i + ahead))
-
-        for copy in pair(i):
-            copy.wait()
-        return clipped(gate_w[i], bg[i]), clipped(up_w[i], bu[i])
-
+    total = scatter_sum(chips, part, near_1, slot_1, far_1, *links[4:8])
+    unroll_tokens(teacher[...].astype(F32), line)
+    res_held[lax.axis_index("hid")] = (total - line[...]).astype(BF16)
+    line[...] = total
+    roll_tokens(line, student)
+    gather_blocks(chips, res_held, *links[8:12])
+    to_rows(res_held, flat, res_rows)
     backward_products(
-        steps, cut, tiles, rows, (gate_w, up_w, down_w), gate_pre, up_pre, d_hidden, d_gate, d_up,
-        flat, ready_down, ready_pair,
+        steps, cut, tiles, res_rows, held_w, gate_pre, up_pre, d_hidden, d_gate, d_up, flat,
+        lambda c: down_w[c],
+        lambda i: (gate_w[i], up_w[i]),
     )
     to_shares(flat, part)
+    line[...] = scatter_sum(chips, part, near_2, slot_2, far_2, *links[12:16])
+    roll_tokens(line, token_grad)
 
 
 def outer(left, right, mask, out):
@@ -403,20 +342,18 @@
         ).astype(BF16)
 
 
-def grad_kernel(tok, res, hidden, d_gate, d_up, mask, gg, gu, gd, flat, rows, rows2, mg, mu, md):
+def grad_kernel(rows, res_rows, hidden, d_gate, d_up, mask, gg, gu, gd, mg, mu, md):
     i = pl.program_id(0)
 
     @pl.when(i == 0)
     def _():
-        to_rows(tok, flat, rows)
-        to_rows(res, flat, rows2)
         spread_rows(mask[0].astype(F32).astype(BF16), mg)
         spread_rows(mask[1].astype(F32).astype(BF16), mu)
         spread_columns(mask[2].astype(F32).astype(BF16), md)
 
     outer(rows[i], d_gate[...], mg[i], gg)
     outer(rows[i], d_up[...], mu[i], gu)
-    outer(hidden[...], rows2[i], md[i], gd)
+    outer(hidden[...], res_rows[i], md[i], gd)
 
 
 def per_device(n, tokens, teacher, w_gate, w_up, w_down, tile_scale, block_mask, bit_width):
@@ -433,84 +370,45 @@
 
     block = jax.ShapeDtypeStruct((mine, width), BF16)
     line = pltpu.VMEM((share, BLOCK), F32)
-    blocks = jax.ShapeDtypeStruct((n, share, BLOCK), BF16)
     held = pltpu.VMEM((n, share, BLOCK), BF16)
     some = pltpu.VMEM((chips, share, BLOCK), BF16)
-
-    tok = exchange(
-        functools.partial(gather_kernel, chips),
-        (tokens,),
-        blocks,
-        [held, line] + link_sems(chips),
-        0,
-    ).reshape(all_tokens, tiles, BLOCK)
-
-    whole = lambda shape: pl.BlockSpec(shape, lambda i: (0,) * len(shape))
-    tok_spec = whole((all_tokens, tiles, BLOCK))
-    pre_spec = whole((all_tokens, hid))
-    part_shape = (2, chips, share, BLOCK)
-    bound_spec = whole((3, hid_tiles, tiles))
     flat = pltpu.VMEM((all_tokens * tiles, BLOCK), F32)
-    rows = pltpu.VMEM((steps, all_tokens, cut), BF16)
     row_tiles = pltpu.VMEM((steps, per, hid), F32)
     column_tiles = pltpu.VMEM((steps, hid_tiles, cut), F32)
-    params = pltpu.CompilerParams(
-        dimension_semantics=("arbitrary",), vmem_limit_bytes=VMEM_BYTES
-    )
-    pre = jax.ShapeDtypeStruct((all_tokens, hid), F32)
+    pre = pltpu.VMEM((all_tokens, hid), F32)
     low = jax.ShapeDtypeStruct((all_tokens, hid), BF16)
-
+    rows = jax.ShapeDtypeStruct((steps, all_tokens, cut), BF16)
     anywhere = pl.BlockSpec(memory_space=pl.ANY)
     vmem = pl.BlockSpec(memory_space=pltpu.VMEM)
     smem = pl.BlockSpec(memory_space=pltpu.SMEM)
-    plain = pltpu.CompilerParams(vmem_limit_bytes=VMEM_BYTES)
-    stores = [
-        pltpu.VMEM((steps, cut, hid), BF16),
-        pltpu.VMEM((steps, cut, hid), BF16),
-        pltpu.VMEM((steps, hid, cut), BF16),
-        pltpu.SemaphoreType.DMA((3, steps)),
-    ]
-    part, gate_pre, up_pre, hidden = pl.pallas_call(
-        functools.partial(forward_kernel, steps, cut, tiles),
-        in_specs=[smem, vmem, anywhere, anywhere, anywhere, vmem, vmem],
-        out_specs=[vmem] * 4,
-        out_shape=[jax.ShapeDtypeStruct(part_shape, BF16), pre, pre, low],
-        scratch_shapes=[flat, rows, row_tiles, row_tiles, column_tiles] + stores,
-        compiler_params=plain,
-    )(bit_width, tok, w_gate, w_up, w_down, tile_scale, block_mask)
-
-    student, res = exchange(
-        functools.partial(residual_kernel, chips),
-        (part, teacher),
-        (block, blocks),
-        [held, some, some, some, line] + link_sems(chips) + link_sems(chips),
-        1,
-    )
-    res = res.reshape(all_tokens, tiles, BLOCK)
-
-    part, d_gate, d_up = pl.pallas_call(
-        functools.partial(backward_kernel, steps, cut, tiles),
-        in_specs=[smem, vmem, anywhere, anywhere, anywhere, vmem, vmem, vmem, vmem],
-        out_specs=[vmem] * 3,
-        out_shape=[jax.ShapeDtypeStruct(part_shape, BF16), low, low],
-        scratch_shapes=[flat, rows, row_tiles, row_tiles, column_tiles]
-        + stores
-        + [pltpu.VMEM((all_tokens, hid), F32)],
-        compiler_params=plain,
-    )(bit_width, res, w_gate, w_up, w_down, tile_scale, block_mask, gate_pre, up_pre)
-
-    token_grad = exchange(
-        functools.partial(scatter_kernel, chips),
-        (part,),
-        block,
-        [some, some, some, line] + link_sems(chips),
-        2,
-    )
-
+
+    student, token_grad, tok_rows, res_rows, hidden, d_gate, d_up = pl.pallas_call(
+        functools.partial(layer_kernel, chips, steps, cut, tiles),
+        in_specs=[smem, vmem, vmem, anywhere, anywhere, anywhere, vmem, vmem],
+        out_specs=[vmem] * 7,
+        out_shape=[block, block, rows, rows, low, low, low],
+        scratch_shapes=[
+            pltpu.VMEM((steps, cut, hid), BF16),
+            pltpu.VMEM((steps, cut, hid), BF16),
+            pltpu.VMEM((steps, hid, cut), BF16),
+            pltpu.SemaphoreType.DMA((3, steps)),
+            flat, row_tiles, row_tiles, column_tiles, pre, pre, pre, line,
+            pltpu.VMEM((2, chips, share, BLOCK), BF16),
+            held, some, some, some, held, some, some, some,
+        ]
+        + link_sems(chips) * 4,
+        compiler_params=pltpu.CompilerParams(
+            collective_id=0, has_side_effects=True, vmem_limit_bytes=VMEM_BYTES
+        ),
+    )(bit_width, tokens, teacher, w_gate, w_up, w_down, tile_scale, block_mask)
+
+    whole = lambda shape: pl.BlockSpec(shape, lambda i: (0,) * len(shape))
+    pre_spec = whole((all_tokens, hid))
+    row_spec = whole((steps, all_tokens, cut))
     grad_gate, grad_up, grad_down = pl.pallas_call(
         grad_kernel,
         grid=(steps,),
-        in_specs=[tok_spec, tok_spec, pre_spec, pre_spec, pre_spec, bound_spec],
+        in_specs=[row_spec, row_spec, pre_spec, pre_spec, pre_spec, whole(block_mask.shape)],
         out_specs=[
             pl.BlockSpec((cut, hid), lambda i: (i, 0)),
             pl.BlockSpec((cut, hid), lambda i: (i, 0)),
@@ -521,9 +419,11 @@
             jax.ShapeDtypeStruct((width, hid), BF16),
             jax.ShapeDtypeStruct((hid, width), BF16),
         ],
-        scratch_shapes=[flat, rows, rows, row_tiles, row_tiles, column_tiles],
-        compiler_params=params,
-    )(tok, res, hidden, d_gate, d_up, block_mask)
+        scratch_shapes=[row_tiles, row_tiles, column_tiles],
+        compiler_params=pltpu.CompilerParams(
+            dimension_semantics=("arbitrary",), vmem_limit_bytes=VMEM_BYTES
+        ),
+    )(tok_rows, res_rows, hidden, d_gate, d_up, block_mask)
 
     return (
         student,

time: 99.2 us -> 83.1 us (0.84)
  Pallas kernels: 96.2 us -> 79.3 us
    pallas_call x6 -> x2, Pallas kernels: 96.2 us -> 79.3 us  [the longest x1 60.4 us: per_device(): pl.pallas_call(functools.partial(layer_kernel, chips, steps, cut, tiles),...]
    unnamed x4 -> x2, local copies, waits for them, and re-layouts: 2.02 us -> 2.81 us
where the time goes in v2:
time: 83.1 us; the launch traced here: 82.7 us
  Pallas kernels  79.3 us (95%)
  local copies, waits for them, and re-layouts  2.81 us (3%)
    pallas_call x1, Pallas kernels, per_device(): pl.pallas_call(functools.partial(layer_kernel, chips, steps, cut, tiles),...  60.4 us
    pallas_call x1, Pallas kernels, per_device(): pl.pallas_call(grad_kernel, grid=(steps,), in_specs=[row_spec, row_spec,...  18.9 us
    unnamed x2, local copies, waits for them, and re-layouts  2.81 us

profile of v2, /device:TPU:0, one launch (start us, length us, event | category | flops | bytes accessed | tf_op | source)
XLA Modules:
  0.0 82.7 jit_solution(10706205016877080589)
XLA Ops:
  0.6 60.4 %shard_map.119 = (bf16[1,8192]{1,0:T(2,128)(2,1)}, bf16[1,8192]{1,0:T(2,128)(2,1)}, bf16[8,16,1024]{2,1,0:T(8,128)(2,1)}, bf16[8,16,1024]{2,1,0:T(8,128)(2,1)}, ...) custom-call(s32[3]{0:T(128)} %width.1, bf16[1,8192]{1,0:T(2,128)(2,1)} %tokens.1, ...), custom_call_target="tpu_custom_call" | custom-call | tf_op jit(solution)/shard_map/pallas_call | solution.py:385
  61.1 18.9 %shard_map.120 = (bf16[8192,1024]{1,0:T(8,128)(2,1)}, bf16[8192,1024]{1,0:T(8,128)(2,1)}, bf16[1024,8192]{1,0:T(8,128)(2,1)}) custom-call(bf16[8,16,1024]{2,1,0:T(8,128)(2,1)} %get-tuple-element.17.rows, bf16[8,16,1024]{2,1,0:T(8,128)(2,1)} %get-tuple-element.18.res_rows, bf16[16,1024]{1,0:T(8,128)(2,1)} %get-tuple-element.19.hidden, ...), custom_call_target="tpu_custom_call" | custom-call | tf_op jit(solution)/shard_map/pallas_call | solution.py:408
  79.9 1.4 %copy.15 = bf16[1,8192]{1,0:T(2,128)(2,1)} copy(bf16[1,8192]{1,0:T(2,128)(2,1)} %get-tuple-element.30) | data formatting | bytes 32768
  81.3 1.4 %copy.16 = bf16[1,8192]{1,0:T(2,128)(2,1)} copy(bf16[1,8192]{1,0:T(2,128)(2,1)} %get-tuple-element.31) | data formatting | bytes 32768
